TPU v7x, 32 devices: a whole 2x2x4 slice. The times are simulated.
32 devices in a mesh: row: 4 (over x, core), col: 8 (over z, y).
Axes of the slice: x: 2, y: 2, z: 4, core: 2. Of those that a mesh axis runs over, the one named last changes fastest.
Arguments:
- basis: bfloat16 [8192, 256], P(('row', 'col')), may hold values from -6 to 6
- degree_scale: float32 [8192], P(('row', 'col')), may hold values from 0.5 to 3
- tile_data: bfloat16 [64, 8, 8, 128, 128], P('row', 'col'), may hold values from -0.125 to 0.125
- tile_index: int32 [64, 8, 8], P('row', 'col'), may hold values from 0 to 7, as said below
- tile_count: int32 [64, 8], P('row', 'col'), may hold values from 1 to 8, as said below
Outputs:
- embedding: float32 [8192, 256], P(('row', 'col'))
- factor: float32 [256, 256], replicated
Inputs may be any that keep to these rules, and one draw needn't show every extreme that they name: `tile_index`: all 8 entries of one tile row in one column block are distinct. `tile_count`: some tile row has 8 live slots in every draw; loads differ widely between devices.
All inputs are finite; a program needn't handle non-finite values.
Results may differ from a plain program's by a relative error of at most 0.034.
Values may be sent and summed in bfloat16 or wider, within the bound.
A program may use at most 128 MiB of HBM per device.

v0:
```python
import jax
import jax.numpy as jnp
from jax import lax
from jax.sharding import PartitionSpec as P

ITERS = 4


def gram_of(image, nodes):
    return (
        lax.dot_general(
            image,
            image,
            (((0,), (0,)), ((), ())),
            precision=lax.Precision.HIGHEST,
            preferred_element_type=jnp.float32,
        )
        / nodes
    )


def normalize(image, gram):
    lower = jnp.linalg.cholesky(gram)
    solved = jax.scipy.linalg.solve_triangular(lower, image.T, lower=True).T
    return (solved, lower.T)


def body(basis, degree_scale, tile_data, tile_index, tile_count):
    tiles = tile_data[:, 0]
    index = tile_index[:, 0]
    counts = tile_count[:, 0]
    rows_dev, width = basis.shape
    tile = tiles.shape[-1]
    slots = tiles.shape[1]
    nodes = rows_dev * lax.axis_size("row") * lax.axis_size("col")
    live = jnp.arange(slots)[None, :] < counts[:, None]
    scale = degree_scale[:, None]
    probe = (basis.astype(jnp.float32) * scale).astype(jnp.bfloat16)
    block_basis, block_degree = (
        lax.all_gather(probe, "row", axis=0, tiled=True),
        lax.all_gather(degree_scale.astype(jnp.bfloat16), "row", axis=0, tiled=True).astype(
            degree_scale.dtype
        ),
    )
    block_scale = block_degree[:, None]
    own_start = lax.axis_index("row") * rows_dev
    block_embedding = None
    factor = None
    for step in range(ITERS):
        tiled = block_basis.reshape(-1, tile, width)
        number = lax.axis_size("col") * rows_dev // tile
        chosen = jnp.where(live[:, :, None, None], tiled[index], jnp.zeros((), jnp.bfloat16))
        result = lax.dot_general(
            tiles, chosen, (((1, 3), (1, 2)), ((0,), (0,))), preferred_element_type=jnp.float32
        )
        summed = lax.psum_scatter(
            result.reshape(number * tile, width).astype(jnp.bfloat16),
            "col",
            scatter_dimension=0,
            tiled=True,
        ).astype(jnp.float32)
        image = summed * scale
        block_image = lax.all_gather(image.astype(jnp.bfloat16), "row", axis=0, tiled=True).astype(
            image.dtype
        )
        gram = lax.psum(gram_of(block_image, nodes).astype(jnp.bfloat16), "col").astype(jnp.float32)
        block_embedding, factor = normalize(block_image, gram)
        block_basis = (block_embedding * block_scale).astype(jnp.bfloat16)
    embedding = lax.dynamic_slice_in_dim(block_embedding, own_start, rows_dev, 0)
    return (embedding, factor)


def solution(mesh):
    placed = (
        P(("row", "col"), None),
        P(("row", "col")),
        P("row", "col", None, None, None),
        P("row", "col", None),
        P("row", "col"),
    )
    return jax.shard_map(
        body, mesh=mesh, in_specs=placed, out_specs=(P(("row", "col"), None), P()), check_vma=False
    )
```

profile of v0, /device:TPU:0, one launch (start us, length us, event | category | flops | bytes accessed | tf_op | source)
XLA Modules:
  0.0 908.2 jit_solution(12719105985688582903)
XLA Ops:
  9.8 8.6 all_gather.18
  19.4 6.5 gather_fusion
  25.9 6.3 bitcast_convert_fusion.3
  32.3 1.4 copy.58
  33.8 5.1 all-gather
  38.9 59.8 %reduce-scatter.5.cloned.1.call-done = bf16[256,256]{0,1:T(8,128)(2,1)} async-done(((bf16[2048,256]{0,1:T(8,128)(2,1)}), bf16[256,256]{0,1:T(8,128)(2,1)}) %reduce-scatter.5.cloned.1.call-update) | async-done | bytes 131088 | tf_op jit(solution)/shard_map/reduce_scatter | solution.py:56
  99.6 7.1 all_gather.19
  108.1 67.8 %all-reduce.6.cloned.1.call-done = bf16[256,256]{0,1:T(8,128)(2,1)} async-done(((bf16[256,256]{0,1:T(8,128)(2,1)}), bf16[256,256]{0,1:T(8,128)(2,1)}) %all-reduce.6.cloned.1.call-update) | async-done | bytes 131088 | tf_op jit(solution)/shard_map/psum | solution.py:66
  177.9 11.7 %cholesky.214 = f32[128,128]{1,0:T(8,128)S(1)} custom-call(f32[128,128]{1,0:T(8,128)S(1)} %cholesky.346), custom_call_target="Cholesky" | custom-call | tf_op jit(solution)/shard_map/jit(cholesky)/cholesky | solution.py:23
  189.6 9.8 %custom-call.17 = f32[1,128,128]{1,2,0:T(8,128)S(1)} custom-call(f32[1,128,128]{2,1,0:T(8,128)S(1)} %get-tuple-element.99), custom_call_target="InvertDiagBlocksLowerTriangular" | custom-call | tf_op jit(solution)/shard_map/jit(cholesky)/cholesky | solution.py:23
  199.9 11.7 %cholesky.231 = f32[128,128]{1,0:T(8,128)S(1)} custom-call(f32[128,128]{1,0:T(8,128)S(1)} %convolution_subtract_fusion.7), custom_call_target="Cholesky" | custom-call | tf_op jit(solution)/shard_map/jit(cholesky)/cholesky | solution.py:23
  213.9 4.4 while.8
  214.7 1.4 bitcast_dynamic-update-slice_fusion.8
  216.8 1.4 bitcast_dynamic-update-slice_fusion.8
  218.2 19.7 %custom-call.18 = f32[2,128,128]{1,2,0:T(8,128)S(1)} custom-call(f32[2,128,128]{2,1,0:T(8,128)S(1)} %get-tuple-element.30), custom_call_target="InvertDiagBlocksLowerTriangular" | custom-call | tf_op jit(solution)/shard_map/jit(_solve_triangular)/triangular_solve | solution.py:24
  240.1 6.5 gather_fusion.1
  246.7 6.3 bitcast_convert_fusion.2
  253.0 1.4 copy.85
  254.5 63.4 %reduce-scatter.7.cloned.1.call-done = bf16[256,256]{0,1:T(8,128)(2,1)} async-done(((bf16[2048,256]{0,1:T(8,128)(2,1)}), bf16[256,256]{0,1:T(8,128)(2,1)}) %reduce-scatter.7.cloned.1.call-update) | async-done | bytes 131088 | tf_op jit(solution)/shard_map/reduce_scatter | solution.py:56
  318.8 7.1 all_gather.21
  327.6 67.6 %all-reduce.8.cloned.1.call-done = bf16[256,256]{0,1:T(8,128)(2,1)} async-done(((bf16[256,256]{0,1:T(8,128)(2,1)}), bf16[256,256]{0,1:T(8,128)(2,1)}) %all-reduce.8.cloned.1.call-update) | async-done | bytes 131088 | tf_op jit(solution)/shard_map/psum | solution.py:66
  397.1 11.7 %cholesky.248 = f32[128,128]{1,0:T(8,128)S(1)} custom-call(f32[128,128]{1,0:T(8,128)S(1)} %cholesky.349), custom_call_target="Cholesky" | custom-call | tf_op jit(solution)/shard_map/jit(cholesky)/cholesky | solution.py:23
  408.9 9.8 %custom-call.19 = f32[1,128,128]{1,2,0:T(8,128)S(1)} custom-call(f32[1,128,128]{2,1,0:T(8,128)S(1)} %get-tuple-element.95), custom_call_target="InvertDiagBlocksLowerTriangular" | custom-call | tf_op jit(solution)/shard_map/jit(cholesky)/cholesky | solution.py:23
  419.2 11.7 %cholesky.265 = f32[128,128]{1,0:T(8,128)S(1)} custom-call(f32[128,128]{1,0:T(8,128)S(1)} %convolution_subtract_fusion.6), custom_call_target="Cholesky" | custom-call | tf_op jit(solution)/shard_map/jit(cholesky)/cholesky | solution.py:23
  433.7 4.3 while.9
  438.0 19.7 %custom-call.20 = f32[2,128,128]{1,2,0:T(8,128)S(1)} custom-call(f32[2,128,128]{2,1,0:T(8,128)S(1)} %get-tuple-element.31), custom_call_target="InvertDiagBlocksLowerTriangular" | custom-call | tf_op jit(solution)/shard_map/jit(_solve_triangular)/triangular_solve | solution.py:24
  459.9 6.5 gather_fusion.2
  466.4 6.3 bitcast_convert_fusion.1
  472.8 1.4 copy.87
  474.3 63.4 %reduce-scatter.9.cloned.1.call-done = bf16[256,256]{0,1:T(8,128)(2,1)} async-done(((bf16[2048,256]{0,1:T(8,128)(2,1)}), bf16[256,256]{0,1:T(8,128)(2,1)}) %reduce-scatter.9.cloned.1.call-update) | async-done | bytes 131088 | tf_op jit(solution)/shard_map/reduce_scatter | solution.py:56
  538.6 7.1 all_gather.22
  547.1 67.8 %all-reduce.10.cloned.1.call-done = bf16[256,256]{0,1:T(8,128)(2,1)} async-done(((bf16[256,256]{0,1:T(8,128)(2,1)}), bf16[256,256]{0,1:T(8,128)(2,1)}) %all-reduce.10.cloned.1.call-update) | async-done | bytes 131088 | tf_op jit(solution)/shard_map/psum | solution.py:66
  616.9 11.7 %cholesky.282 = f32[128,128]{1,0:T(8,128)S(1)} custom-call(f32[128,128]{1,0:T(8,128)S(1)} %cholesky.352), custom_call_target="Cholesky" | custom-call | tf_op jit(solution)/shard_map/jit(cholesky)/cholesky | solution.py:23
  628.7 9.8 %custom-call.21 = f32[1,128,128]{1,2,0:T(8,128)S(1)} custom-call(f32[1,128,128]{2,1,0:T(8,128)S(1)} %get-tuple-element.91), custom_call_target="InvertDiagBlocksLowerTriangular" | custom-call | tf_op jit(solution)/shard_map/jit(cholesky)/cholesky | solution.py:23
  639.0 11.7 %cholesky.299 = f32[128,128]{1,0:T(8,128)S(1)} custom-call(f32[128,128]{1,0:T(8,128)S(1)} %convolution_subtract_fusion.5), custom_call_target="Cholesky" | custom-call | tf_op jit(solution)/shard_map/jit(cholesky)/cholesky | solution.py:23
  653.5 4.5 while.10
  658.0 19.7 %custom-call.22 = f32[2,128,128]{1,2,0:T(8,128)S(1)} custom-call(f32[2,128,128]{2,1,0:T(8,128)S(1)} %get-tuple-element.32), custom_call_target="InvertDiagBlocksLowerTriangular" | custom-call | tf_op jit(solution)/shard_map/jit(_solve_triangular)/triangular_solve | solution.py:24
  679.9 6.5 gather_fusion.3
  686.4 6.3 bitcast_convert_fusion
  692.8 1.4 copy.89
  694.3 63.3 %reduce-scatter.11.cloned.1.call-done = bf16[256,256]{0,1:T(8,128)(2,1)} async-done(((bf16[2048,256]{0,1:T(8,128)(2,1)}), bf16[256,256]{0,1:T(8,128)(2,1)}) %reduce-scatter.11.cloned.1.call-update) | async-done | bytes 131088 | tf_op jit(solution)/shard_map/reduce_scatter | solution.py:56
  758.5 7.3 all_gather.23
  767.0 68.1 %all-reduce.12.cloned.1.call-done = bf16[256,256]{0,1:T(8,128)(2,1)} async-done(((bf16[256,256]{0,1:T(8,128)(2,1)}), bf16[256,256]{0,1:T(8,128)(2,1)}) %all-reduce.12.cloned.1.call-update) | async-done | bytes 131088 | tf_op jit(solution)/shard_map/psum | solution.py:66
  837.0 11.7 %cholesky.316 = f32[128,128]{1,0:T(8,128)S(1)} custom-call(f32[128,128]{1,0:T(8,128)S(1)} %cholesky.355), custom_call_target="Cholesky" | custom-call | tf_op jit(solution)/shard_map/jit(cholesky)/cholesky | solution.py:23
  848.8 9.8 %custom-call.23 = f32[1,128,128]{1,2,0:T(8,128)S(1)} custom-call(f32[1,128,128]{2,1,0:T(8,128)S(1)} %get-tuple-element.87), custom_call_target="InvertDiagBlocksLowerTriangular" | custom-call | tf_op jit(solution)/shard_map/jit(cholesky)/cholesky | solution.py:23
  859.1 11.7 %cholesky.333 = f32[128,128]{1,0:T(8,128)S(1)} custom-call(f32[128,128]{1,0:T(8,128)S(1)} %convolution_subtract_fusion.4), custom_call_target="Cholesky" | custom-call | tf_op jit(solution)/shard_map/jit(cholesky)/cholesky | solution.py:23
  873.6 4.3 while.11
  877.9 19.7 %custom-call.24 = f32[2,128,128]{1,2,0:T(8,128)S(1)} custom-call(f32[2,128,128]{2,1,0:T(8,128)S(1)} %get-tuple-element.33), custom_call_target="InvertDiagBlocksLowerTriangular" | custom-call | tf_op jit(solution)/shard_map/jit(_solve_triangular)/triangular_solve | solution.py:24
  (133 shorter events, 51.4 us)
Async XLA Ops:
  7.2 91.5 %reduce-scatter.5.cloned.1.call-start = ((), (), s32[]{:S(2)}) async-start(), calls=%async_computation.4 | async-start | bytes 1179648 | tf_op jit(solution)/shard_map/reduce_scatter | solution.py:56
  25.9 7.9 copy-start
  33.7 142.2 %all-reduce.6.cloned.1.call-start = ((), (), s32[]{:S(2)}) async-start(), calls=%async_computation.5 | async-start | bytes 262144 | tf_op jit(solution)/shard_map/psum | solution.py:66
  107.7 210.1 %reduce-scatter.7.cloned.1.call-start = ((), (), s32[]{:S(2)}) async-start(), calls=%async_computation.6 | async-start | bytes 1179648 | tf_op jit(solution)/shard_map/reduce_scatter | solution.py:56
  254.5 140.7 %all-reduce.8.cloned.1.call-start = ((), (), s32[]{:S(2)}) async-start(), calls=%async_computation.7 | async-start | bytes 262144 | tf_op jit(solution)/shard_map/psum | solution.py:66
  327.0 210.7 %reduce-scatter.9.cloned.1.call-start = ((), (), s32[]{:S(2)}) async-start(), calls=%async_computation.8 | async-start | bytes 1179648 | tf_op jit(solution)/shard_map/reduce_scatter | solution.py:56
  474.2 140.7 %all-reduce.10.cloned.1.call-start = ((), (), s32[]{:S(2)}) async-start(), calls=%async_computation.9 | async-start | bytes 262144 | tf_op jit(solution)/shard_map/psum | solution.py:66
  546.7 210.8 %reduce-scatter.11.cloned.1.call-start = ((), (), s32[]{:S(2)}) async-start(), calls=%async_computation.10 | async-start | bytes 1179648 | tf_op jit(solution)/shard_map/reduce_scatter | solution.py:56
  694.2 140.8 %all-reduce.12.cloned.1.call-start = ((), (), s32[]{:S(2)}) async-start(), calls=%async_computation.11 | async-start | bytes 262144 | tf_op jit(solution)/shard_map/psum | solution.py:66
Sparse Core Ops, SparseCore 0:
  33.8 64.7 reduce-scatter.4
  107.8 68.0 all-reduce.5
  254.6 63.2 reduce-scatter.6
  327.1 68.0 all-reduce.7
  474.3 63.2 reduce-scatter.8
  546.8 68.0 all-reduce.9
  694.3 63.1 reduce-scatter.10
  767.0 68.0 all-reduce.11
where the time goes:
time: 913 us; the launch traced here: 908 us
  waiting for transfers between devices  521 us (57%)
  other arithmetic  227 us (25%)
  local copies, waits for them, and re-layouts  56.1 us (6%)
  blocking collectives  42.4 us (5%)
  matrix products  38.6 us (4%)
  between operations  20.3 us (2%)
    psum x4, waiting for transfers between devices, body(): lax.psum(gram_of(block_image, nodes).astype(jnp.bfloat16), 'col')  271 us
    reduce_scatter x4, waiting for transfers between devices, body(): lax.psum_scatter(result.reshape(number * tile, width).astype(jnp.bfloat16...  250 us
    another operation x27, other arithmetic, normalize(): lower = jnp.linalg.cholesky(gram)  138 us
    another operation x8, other arithmetic, normalize(): solved = jax.scipy.linalg.solve_triangular(lower, image.T, lower=True).T  78.8 us
    all_gather x4, blocking collectives, body(): lax.all_gather(image.astype(jnp.bfloat16), 'row', axis=0, tiled=True)  28.7 us
    gather x4, local copies, waits for them, and re-layouts, body(): tiled[index]  26.2 us
    dot_general x4, matrix products, body(): lax.dot_general(tiles, chosen, (((1, 3), (1, 2)), ((0,), (0,))), preferre...  25.4 us
  transfers between devices with their start and end apart: 8, of which 8 were waited for; matrix products, arithmetic and copies ran while one was open for 0% of the time, Pallas kernels for 0%

commit v1 on v0

v1 whole, which is shorter than its diff:
```python
import functools

import jax
import jax.numpy as jnp
from jax import lax
from jax.experimental import pallas as pl
from jax.experimental.pallas import tpu as pltpu
from jax.sharding import PartitionSpec as P

ITERS = 4
LEAF = 128
STEP = 8
F32 = jnp.float32
BF16 = jnp.bfloat16
EXACT = lax.Precision.HIGHEST
MESH = pl.DeviceIdType.MESH
VMEM_BYTES = 56 * 1024 * 1024


def densify_kernel(index_ref, count_ref, tiles_ref, out_ref):
    row = pl.program_id(0)
    slots, tile = tiles_ref.shape[1], tiles_ref.shape[2]
    out_ref[...] = jnp.zeros_like(out_ref)
    for slot in range(slots):

        @pl.when(slot < count_ref[row])
        def _():
            column = pl.multiple_of(index_ref[row, slot] * tile, tile)
            out_ref[:, pl.ds(column, tile)] = tiles_ref[0, slot]


def densify(tiles, index, counts, columns):
    rows, slots, tile, _ = tiles.shape
    return pl.pallas_call(
        densify_kernel,
        grid_spec=pltpu.PrefetchScalarGridSpec(
            num_scalar_prefetch=2,
            grid=(rows,),
            in_specs=[pl.BlockSpec((1, slots, tile, tile), lambda i, *_: (i, 0, 0, 0))],
            out_specs=pl.BlockSpec((tile, columns), lambda i, *_: (i, 0)),
        ),
        out_shape=jax.ShapeDtypeStruct((rows * tile, columns), BF16),
    )(index, counts, tiles)


def leaf_factor(gram):
    size = gram.shape[0]
    rows = lax.broadcasted_iota(jnp.int32, (size, size), 0)
    lanes = lax.broadcasted_iota(jnp.int32, (size, size), 1)
    eye = (rows == lanes).astype(F32)

    def group(g, state):
        work, left = state
        for j in range(STEP):
            pivot_row = work[j : j + 1, :]
            left_row = left[j : j + 1, :]
            column = jnp.broadcast_to(work[:, j : j + 1], (size, size))
            pivot = column[j : j + 1, :]
            open_rows = (rows > j) & (rows < size - STEP * g)
            ratio = jnp.where(open_rows, column * (1.0 / pivot), 0.0)
            work = work - ratio * pivot_row
            left = left - ratio * left_row
        work = jnp.concatenate([work[STEP:], work[:STEP]], axis=0)
        left = jnp.concatenate([left[STEP:], left[:STEP]], axis=0)
        work = pltpu.roll(work, size - STEP, 1)
        return work, left

    work, left = lax.fori_loop(0, size // STEP, group, (gram, eye))
    diagonal = jnp.sum(work * eye, axis=1, keepdims=True)
    inverse = lax.rsqrt(diagonal)
    upper = jnp.where(rows <= lanes, work * inverse, 0.0)
    return upper, left * inverse


def exact_dot(a, b, dims=((1,), (0,))):
    return lax.dot_general(a, b, (dims, ((), ())), precision=EXACT, preferred_element_type=F32)


def factorize(gram_ref, fac_ref, inv_ref):
    size = gram_ref.shape[0]
    fac_ref[...] = jnp.zeros_like(fac_ref)
    inv_ref[...] = jnp.zeros_like(inv_ref)
    for start in range(0, size, LEAF):
        here = pl.ds(start, LEAF)
        upper, left = leaf_factor(gram_ref[here, here])
        inv = left.T
        fac_ref[here, here] = upper
        rest = size - start - LEAF
        if rest:
            after = pl.ds(start + LEAF, rest)
            panel = exact_dot(left, gram_ref[here, after])
            fac_ref[here, after] = panel
            gram_ref[after, after] = gram_ref[after, after] - exact_dot(panel, panel, ((0,), (0,)))
        if start:
            before = pl.ds(0, start)
            above = exact_dot(fac_ref[before, here], inv)
            inv_ref[before, here] = -exact_dot(inv_ref[before, before], above)
        inv_ref[here, here] = inv


def kernel(
    n_row, n_col, nodes,
    a_ref, basis_ref, scale_ref,
    emb_ref, fac_ref,
    probe, img, scl, srow, rs_out, rs_in, g_out, g_in, g_all, gram, inv, image,
    sc_send, sc_recv, ag_send, ag_recv, rs_send, rs_recv, ga_send, ga_recv, gb_send, gb_recv,
):
    my_row, my_col = lax.axis_index("row"), lax.axis_index("col")
    rows, width = basis_ref.shape
    row_peers = [lax.rem(my_row + d, n_row) for d in range(1, n_row)]
    col_peers = [lax.rem(my_col + d, n_col) for d in range(1, n_col)]
    tile = 128

    barrier = pltpu.get_barrier_semaphore()
    for r in row_peers:
        pl.semaphore_signal(barrier, inc=1, device_id=(r, my_col), device_id_type=MESH)
    for c in col_peers:
        pl.semaphore_signal(barrier, inc=1, device_id=(my_row, c), device_id_type=MESH)
    pl.semaphore_wait(barrier, n_row + n_col - 2)

    def remote(src, dst, send, recv, device):
        return pltpu.make_async_remote_copy(
            src_ref=src, dst_ref=dst, send_sem=send, recv_sem=recv,
            device_id=device, device_id_type=MESH,
        )

    def start_gather(buf, send, recv):
        for r in row_peers:
            remote(buf.at[my_row], buf.at[my_row], send.at[r], recv.at[my_row], (r, my_col)).start()

    def wait_gather(buf, send, recv):
        for r in row_peers:
            remote(buf.at[my_row], buf.at[r], send.at[r], recv.at[r], (r, my_col)).wait()

    def start_cols(src, dst, send, recv, own_src):
        for c in col_peers:
            s = src.at[my_col] if own_src else src.at[c]
            remote(s, dst.at[my_col], send.at[c], recv.at[my_col], (my_row, c)).start()

    def wait_cols(src, dst, send, recv, own_src):
        for c in col_peers:
            s = src.at[my_col] if own_src else src.at[c]
            remote(s, dst.at[c], send.at[c], recv.at[c], (my_row, c)).wait()

    def column_sum(src, par):
        total = src[par, 0].astype(F32)
        for c in range(1, n_col):
            total = total + src[par, c].astype(F32)
        return total

    def scale_of(part):
        block = scl[pl.ds(part * rows if isinstance(part, int) else pl.multiple_of(part * rows, rows), rows), :]
        return jnp.concatenate([block] * (width // 128), axis=1)

    def make_probe(par):
        for r in range(n_row):
            probe[pl.ds(r * rows, rows), :] = (img[par, r].astype(F32) * scale_of(r)).astype(BF16)

    img[1, my_row] = basis_ref[...]
    srow[my_row] = scale_ref[...]
    start_gather(srow, sc_send, sc_recv)
    start_gather(img.at[1], ag_send.at[1], ag_recv.at[1])
    wait_gather(srow, sc_send, sc_recv)
    for r in range(n_row):
        for part in range(rows // tile):
            line = jnp.broadcast_to(srow[r, part : part + 1, :], (tile, tile))
            scl[pl.ds(r * rows + part * tile, tile), :] = line.T
    wait_gather(img.at[1], ag_send.at[1], ag_recv.at[1])
    make_probe(1)

    def gram_start(par):
        whole = img[par, 0]
        total = lax.dot_general(whole, whole, (((0,), (0,)), ((), ())), preferred_element_type=F32)
        for r in range(1, n_row):
            whole = img[par, r]
            total = total + lax.dot_general(
                whole, whole, (((0,), (0,)), ((), ())), preferred_element_type=F32
            )
        total = (total / nodes).astype(BF16)
        piece = width // n_col
        for c in range(n_col):
            g_out[c] = total[c * piece : (c + 1) * piece, :]
        g_in[par, my_col] = g_out[my_col]
        start_cols(g_out, g_in.at[par], ga_send.at[par], ga_recv.at[par], False)

    def gram_middle(par):
        wait_cols(g_out, g_in.at[par], ga_send.at[par], ga_recv.at[par], False)
        g_all[par, my_col] = column_sum(g_in, par).astype(BF16)
        start_cols(g_all.at[par], g_all.at[par], gb_send.at[par], gb_recv.at[par], True)

    def gram_end(par):
        wait_cols(g_all.at[par], g_all.at[par], gb_send.at[par], gb_recv.at[par], True)
        piece = width // n_col
        for c in range(n_col):
            gram[pl.ds(c * piece, piece), :] = g_all[par, c].astype(F32)
        factorize(gram, fac_ref, inv)

    for step in range(ITERS):
        par, last = step % 2, (step + 1) % 2
        if step:
            gram_start(last)

        @pl.loop(0, n_col)
        def _(c):
            block = a_ref[pl.ds(pl.multiple_of(c * rows, rows), rows), :]
            rs_out[c] = jnp.dot(block, probe[...], preferred_element_type=F32).astype(BF16)

        if step:
            gram_middle(last)
        rs_in[par, my_col] = rs_out[my_col]
        start_cols(rs_out, rs_in.at[par], rs_send.at[par], rs_recv.at[par], False)
        if step:
            gram_end(last)
        wait_cols(rs_out, rs_in.at[par], rs_send.at[par], rs_recv.at[par], False)
        own = column_sum(rs_in, par) * scale_of(my_row)
        if step:
            own = exact_dot(own, inv[...])
        image[...] = own
        img[par, my_row] = own.astype(BF16)
        start_gather(img.at[par], ag_send.at[par], ag_recv.at[par])
        wait_gather(img.at[par], ag_send.at[par], ag_recv.at[par])
        if step < ITERS - 1:
            make_probe(par)

    par = (ITERS - 1) % 2
    gram_start(par)
    gram_middle(par)
    gram_end(par)
    emb_ref[...] = exact_dot(image[...], inv[...])


def body(n_row, n_col, basis, degree_scale, tile_data, tile_index, tile_count):
    rows, width = basis.shape
    block = n_row * rows
    dense = densify(tile_data[:, 0], tile_index[:, 0], tile_count[:, 0], block)
    scale = jnp.pad(degree_scale.reshape(-1, 128), ((0, 8 - rows // 128), (0, 0)))
    vmem = pl.BlockSpec(memory_space=pltpu.VMEM)
    dma = pltpu.SemaphoreType.DMA
    piece = width // n_col
    nodes = block * n_col
    return pl.pallas_call(
        functools.partial(kernel, n_row, n_col, nodes),
        out_shape=(
            jax.ShapeDtypeStruct((rows, width), F32),
            jax.ShapeDtypeStruct((width, width), F32),
        ),
        in_specs=[vmem] * 3,
        out_specs=(vmem, vmem),
        scratch_shapes=[
            pltpu.VMEM((block, width), BF16),
            pltpu.VMEM((2, n_row, rows, width), BF16),
            pltpu.VMEM((block, 128), F32),
            pltpu.VMEM((n_row, 8, 128), F32),
            pltpu.VMEM((n_col, rows, width), BF16),
            pltpu.VMEM((2, n_col, rows, width), BF16),
            pltpu.VMEM((n_col, piece, width), BF16),
            pltpu.VMEM((2, n_col, piece, width), BF16),
            pltpu.VMEM((2, n_col, piece, width), BF16),
            pltpu.VMEM((width, width), F32),
            pltpu.VMEM((width, width), F32),
            pltpu.VMEM((rows, width), F32),
            dma((n_row,)), dma((n_row,)), dma((2, n_row)), dma((2, n_row)),
            dma((2, n_col)), dma((2, n_col)), dma((2, n_col)), dma((2, n_col)),
            dma((2, n_col)), dma((2, n_col)),
        ],
        compiler_params=pltpu.CompilerParams(
            collective_id=0, has_side_effects=True, vmem_limit_bytes=VMEM_BYTES
        ),
    )(dense, basis, scale)


def solution(mesh):
    placed = (
        P(("row", "col"), None),
        P(("row", "col")),
        P("row", "col", None, None, None),
        P("row", "col", None),
        P("row", "col"),
    )
    return jax.shard_map(
        functools.partial(body, mesh.shape["row"], mesh.shape["col"]),
        mesh=mesh,
        in_specs=placed,
        out_specs=(P(("row", "col"), None), P()),
        check_vma=False,
    )
```

time: 913 us -> 242 us (0.27)
  waiting for transfers between devices: 521 us -> 0 us
  Pallas kernels: 0 us -> 235 us
  other arithmetic: 227 us -> 0 us
  local copies, waits for them, and re-layouts: 56.1 us -> 5.97 us
  blocking collectives: 42.4 us -> 0 us
  matrix products: 38.6 us -> 0 us
  between operations: 20.3 us -> 0.64 us
    psum x4 -> x0, waiting for transfers between devices: 271 us -> none  [body(): lax.psum(gram_of(block_image, nodes).astype(jnp.bfloat16), 'col')]
    reduce_scatter x4 -> x0, waiting for transfers between devices: 250 us -> none  [body(): lax.psum_scatter(result.reshape(number * tile, width).astype(jnp.bfloat16...]
    pallas_call x0 -> x2, Pallas kernels: none -> 235 us  [the longest x1 224 us: body(): pl.pallas_call(functools.partial(kernel, n_row, n_col, nodes), out_shape=...]
    another operation x35 -> x0, other arithmetic: 217 us -> none  [the longest x27 138 us: normalize(): lower = jnp.linalg.cholesky(gram)]
    all_gather x6 -> x0, blocking collectives: 42.4 us -> none  [the longest x4 28.7 us: body(): lax.all_gather(image.astype(jnp.bfloat16), 'row', axis=0, tiled=True)]
    dot_general x8 -> x0, matrix products: 29.3 us -> none  [the longest x4 25.4 us: body(): lax.dot_general(tiles, chosen, (((1, 3), (1, 2)), ((0,), (0,))), preferre...]
    gather x4 -> x0, local copies, waits for them, and re-layouts: 26.2 us -> none  [body(): tiled[index]]
    another operation x37 -> x0, local copies, waits for them, and re-layouts: 16.4 us -> none  [the longest x29 16.3 us: normalize(): solved = jax.scipy.linalg.solve_triangular(lower, image.T, lower=True).T]
  transfers between devices with their start and end apart: 8 -> 0, of which waited for: 8 -> 0; matrix products, arithmetic and copies ran while one was open for 0% -> 0% of each run, Pallas kernels for 0% -> 0%
where the time goes in v1:
time: 242 us
  Pallas kernels  235 us (97%)
  local copies, waits for them, and re-layouts  5.97 us (2%)
    pallas_call x1, Pallas kernels, body(): pl.pallas_call(functools.partial(kernel, n_row, n_col, nodes), out_shape=...  224 us
    pallas_call x1, Pallas kernels, densify(): pl.pallas_call(densify_kernel, grid_spec=pltpu.PrefetchScalarGridSpec(num...  11.4 us

profile of v1, /device:TPU:0, one launch (start us, length us, event | category | flops | bytes accessed | tf_op | source)
XLA Modules:
  0.0 241.6 jit_solution(13822947576907825918)
XLA Ops:
  0.6 1.3 pad.4.scale_ref
  1.9 1.4 copy.7.index_ref
  3.3 11.4 %shard_map.68.a_ref = bf16[2048,1024]{1,0:T(8,128)(2,1)} custom-call(s32[16,8]{1,0:T(8,128)} %copy.7.index_ref, s32[16]{0:T(128)} %bitcast.7, bf16[16,8,128,128]{3,2,1,0:T(8,128)(2,1)} %bitcast.4), custom_call_target="tpu_custom_call" | custom-call | tf_op jit(solution)/shard_map/pallas_call | solution.py:34
  14.6 223.6 %shard_map.69 = (f32[256,256]{1,0:T(8,128)}, f32[256,256]{1,0:T(8,128)}) custom-call(bf16[2048,1024]{1,0:T(8,128)(2,1)} %shard_map.68.a_ref, bf16[256,256]{1,0:T(8,128)(2,1)} %basis_ref.1, f32[8,128]{1,0:T(8,128)} %pad.4.scale_ref), custom_call_target="tpu_custom_call" | custom-call | tf_op jit(solution)/shard_map/pallas_call | solution.py:241
  238.2 1.7 copy.10
  239.9 1.7 copy.11

commit v2 on v1

--- a/solution.py
+++ b/solution.py
@@ -17,30 +17,21 @@
 VMEM_BYTES = 56 * 1024 * 1024
 
 
-def densify_kernel(index_ref, count_ref, tiles_ref, out_ref):
-    row = pl.program_id(0)
-    slots, tile = tiles_ref.shape[1], tiles_ref.shape[2]
-    out_ref[...] = jnp.zeros_like(out_ref)
-    for slot in range(slots):
-
-        @pl.when(slot < count_ref[row])
-        def _():
-            column = pl.multiple_of(index_ref[row, slot] * tile, tile)
-            out_ref[:, pl.ds(column, tile)] = tiles_ref[0, slot]
-
-
-def densify(tiles, index, counts, columns):
-    rows, slots, tile, _ = tiles.shape
-    return pl.pallas_call(
-        densify_kernel,
-        grid_spec=pltpu.PrefetchScalarGridSpec(
-            num_scalar_prefetch=2,
-            grid=(rows,),
-            in_specs=[pl.BlockSpec((1, slots, tile, tile), lambda i, *_: (i, 0, 0, 0))],
-            out_specs=pl.BlockSpec((tile, columns), lambda i, *_: (i, 0)),
-        ),
-        out_shape=jax.ShapeDtypeStruct((rows * tile, columns), BF16),
-    )(index, counts, tiles)
+def densify(tiles_ref, index_ref, count_ref, dense):
+    trows, slots, tile, _ = tiles_ref.shape
+
+    @pl.loop(0, trows)
+    def _(t):
+        here = pl.ds(pl.multiple_of(t * tile, tile), tile)
+        for column in range(dense.shape[1] // tile):
+            slot, live = jnp.int32(0), jnp.float32(0.0)
+            for s in range(slots):
+                hit = (index_ref[t, s] == column) & (s < count_ref[t, 0])
+                slot = jnp.where(hit, s, slot)
+                live = jnp.where(hit, 1.0, live)
+            dense[here, pl.ds(column * tile, tile)] = (
+                tiles_ref[t, slot].astype(F32) * live
+            ).astype(BF16)
 
 
 def leaf_factor(gram):
@@ -49,19 +40,39 @@
     lanes = lax.broadcasted_iota(jnp.int32, (size, size), 1)
     eye = (rows == lanes).astype(F32)
 
+    sub = lax.broadcasted_iota(jnp.int32, (STEP, size), 0)
+
+    def combine(factors, panel):
+        total = factors[0] * panel[0:1, :]
+        for k in range(1, STEP):
+            total = total + factors[k] * panel[k : k + 1, :]
+        return total
+
     def group(g, state):
         work, left = state
+        cols = [jnp.broadcast_to(work[:, j : j + 1], (size, size)) for j in range(STEP)]
+        block = [c[:STEP] for c in cols]
+        lower = [(sub == j).astype(F32) for j in range(STEP)]
+        full = list(lower)
+        scale = jnp.ones((STEP, size), F32)
         for j in range(STEP):
-            pivot_row = work[j : j + 1, :]
-            left_row = left[j : j + 1, :]
-            column = jnp.broadcast_to(work[:, j : j + 1], (size, size))
-            pivot = column[j : j + 1, :]
-            open_rows = (rows > j) & (rows < size - STEP * g)
-            ratio = jnp.where(open_rows, column * (1.0 / pivot), 0.0)
-            work = work - ratio * pivot_row
-            left = left - ratio * left_row
-        work = jnp.concatenate([work[STEP:], work[:STEP]], axis=0)
-        left = jnp.concatenate([left[STEP:], left[:STEP]], axis=0)
+            over = 1.0 / block[j][j : j + 1, :]
+            ratio = jnp.where(sub == j, 0.0, block[j] * over)
+            below = jnp.where(sub > j, ratio, 0.0)
+            scale = jnp.where(sub == j, over, scale)
+            for k in range(j + 1, STEP):
+                block[k] = block[k] - ratio * block[k][j : j + 1, :]
+            for k in range(j + 1):
+                lower[k] = lower[k] - below * lower[k][j : j + 1, :]
+                full[k] = full[k] - ratio * full[k][j : j + 1, :]
+        full = [f * scale for f in full]
+        work_panel, left_panel = work[:STEP], left[:STEP]
+        open_rows = rows[STEP:] < size - STEP * g
+        cols = [jnp.where(open_rows, c[STEP:], 0.0) for c in cols]
+        work_rest = work[STEP:] - combine(cols, combine(full, work_panel))
+        left_rest = left[STEP:] - combine(cols, combine(full, left_panel))
+        work = jnp.concatenate([work_rest, combine(lower, work_panel)], axis=0)
+        left = jnp.concatenate([left_rest, combine(lower, left_panel)], axis=0)
         work = pltpu.roll(work, size - STEP, 1)
         return work, left
 
@@ -100,9 +111,9 @@
 
 def kernel(
     n_row, n_col, nodes,
-    a_ref, basis_ref, scale_ref,
+    tiles_ref, index_ref, count_ref, basis_ref, scale_ref,
     emb_ref, fac_ref,
-    probe, img, scl, srow, rs_out, rs_in, g_out, g_in, g_all, gram, inv, image,
+    a_ref, probe, img, scl, srow, rs_out, rs_in, g_out, g_in, g_all, gram, inv, image,
     sc_send, sc_recv, ag_send, ag_recv, rs_send, rs_recv, ga_send, ga_recv, gb_send, gb_recv,
 ):
     my_row, my_col = lax.axis_index("row"), lax.axis_index("col")
@@ -160,6 +171,7 @@
     srow[my_row] = scale_ref[...]
     start_gather(srow, sc_send, sc_recv)
     start_gather(img.at[1], ag_send.at[1], ag_recv.at[1])
+    densify(tiles_ref, index_ref, count_ref, a_ref)
     wait_gather(srow, sc_send, sc_recv)
     for r in range(n_row):
         for part in range(rows // tile):
@@ -232,9 +244,9 @@
 def body(n_row, n_col, basis, degree_scale, tile_data, tile_index, tile_count):
     rows, width = basis.shape
     block = n_row * rows
-    dense = densify(tile_data[:, 0], tile_index[:, 0], tile_count[:, 0], block)
     scale = jnp.pad(degree_scale.reshape(-1, 128), ((0, 8 - rows // 128), (0, 0)))
     vmem = pl.BlockSpec(memory_space=pltpu.VMEM)
+    smem = pl.BlockSpec(memory_space=pltpu.SMEM)
     dma = pltpu.SemaphoreType.DMA
     piece = width // n_col
     nodes = block * n_col
@@ -244,9 +256,10 @@
             jax.ShapeDtypeStruct((rows, width), F32),
             jax.ShapeDtypeStruct((width, width), F32),
         ),
-        in_specs=[vmem] * 3,
+        in_specs=[vmem, smem, smem, vmem, vmem],
         out_specs=(vmem, vmem),
         scratch_shapes=[
+            pltpu.VMEM((tile_data.shape[0] * tile_data.shape[-1], block), BF16),
             pltpu.VMEM((block, width), BF16),
             pltpu.VMEM((2, n_row, rows, width), BF16),
             pltpu.VMEM((block, 128), F32),
@@ -266,7 +279,7 @@
         compiler_params=pltpu.CompilerParams(
             collective_id=0, has_side_effects=True, vmem_limit_bytes=VMEM_BYTES
         ),
-    )(dense, basis, scale)
+    )(tile_data[:, 0], tile_index[:, 0], tile_count, basis, scale)
 
 
 def solution(mesh):

time: 242 us -> 199 us (0.82)
  Pallas kernels: 235 us -> 191 us
    pallas_call x1, Pallas kernels: 224 us -> 191 us  [body(): pl.pallas_call(functools.partial(kernel, n_row, n_col, nodes), out_shape=...]
    pallas_call x1 -> x0, Pallas kernels: 11.4 us -> none  [densify(): pl.pallas_call(densify_kernel, grid_spec=pltpu.PrefetchScalarGridSpec(num...]
where the time goes in v2:
time: 199 us
  Pallas kernels  191 us (96%)
  local copies, waits for them, and re-layouts  7.29 us (4%)
    pallas_call x1, Pallas kernels, body(): pl.pallas_call(functools.partial(kernel, n_row, n_col, nodes), out_shape=...  191 us
    unnamed x3, local copies, waits for them, and re-layouts  4.67 us

profile of v2, /device:TPU:0, one launch (start us, length us, event | category | flops | bytes accessed | tf_op | source)
XLA Modules:
  0.0 198.9 jit_solution(375863976274998386)
XLA Ops:
  0.6 1.3 pad.4.scale_ref
  1.9 1.4 copy.7.index_ref
  3.3 1.3 copy.8.count_ref
  4.6 191.0 %shard_map.68 = (f32[256,256]{1,0:T(8,128)}, f32[256,256]{1,0:T(8,128)}) custom-call(bf16[16,8,128,128]{3,2,1,0:T(8,128)(2,1)} %bitcast.3, s32[16,8]{1,0:T(8,128)} %copy.7.index_ref, s32[16,1]{1,0:T(8,128)} %copy.8.count_ref, bf16[256,256]{1,0:T(8,128)(2,1)} %basis_ref.1, f32[8,128]{1,0:T(8,128)} %pad.4.scale_ref), custom_call_target="tpu_custom_call" | custom-call | tf_op jit(solution)/shard_map/pallas_call | solution.py:253
  195.6 1.7 copy.11
  197.3 1.7 copy.12

commit v3 on v2

--- a/solution.py
+++ b/solution.py
@@ -9,6 +9,7 @@
 
 ITERS = 4
 LEAF = 128
+DEEP = 4
 STEP = 8
 F32 = jnp.float32
 BF16 = jnp.bfloat16
@@ -87,11 +88,12 @@
     return lax.dot_general(a, b, (dims, ((), ())), precision=EXACT, preferred_element_type=F32)
 
 
-def factorize(gram_ref, fac_ref, inv_ref):
+def factorize(gram_ref, fac_ref, inv_ref, starts):
     size = gram_ref.shape[0]
-    fac_ref[...] = jnp.zeros_like(fac_ref)
-    inv_ref[...] = jnp.zeros_like(inv_ref)
-    for start in range(0, size, LEAF):
+    for start in starts:
+        if not start:
+            fac_ref[...] = jnp.zeros_like(fac_ref)
+            inv_ref[...] = jnp.zeros_like(inv_ref)
         here = pl.ds(start, LEAF)
         upper, left = leaf_factor(gram_ref[here, here])
         inv = left.T
@@ -113,14 +115,18 @@
     n_row, n_col, nodes,
     tiles_ref, index_ref, count_ref, basis_ref, scale_ref,
     emb_ref, fac_ref,
-    a_ref, probe, img, scl, srow, rs_out, rs_in, g_out, g_in, g_all, gram, inv, image,
-    sc_send, sc_recv, ag_send, ag_recv, rs_send, rs_recv, ga_send, ga_recv, gb_send, gb_recv,
+    a_ref, probe, img, scl, srow, rs_out, rs_in, g_out, g_in, g_all, gram, inv, image, s2_out, s2_in,
+    sc_send, sc_recv, ag_send, ag_recv, rs_send, rs_recv, ga_send, ga_recv, gb_send, gb_recv, s2_send, s2_recv,
 ):
     my_row, my_col = lax.axis_index("row"), lax.axis_index("col")
     rows, width = basis_ref.shape
     row_peers = [lax.rem(my_row + d, n_row) for d in range(1, n_row)]
     col_peers = [lax.rem(my_col + d, n_col) for d in range(1, n_col)]
     tile = 128
+    deep = min(DEEP, n_col)
+    wide = n_col // deep
+    my_z, my_y = my_col // wide, lax.rem(my_col, wide)
+    starts = list(range(0, width, LEAF))
 
     barrier = pltpu.get_barrier_semaphore()
     for r in row_peers:
@@ -205,7 +211,36 @@
         piece = width // n_col
         for c in range(n_col):
             gram[pl.ds(c * piece, piece), :] = g_all[par, c].astype(F32)
-        factorize(gram, fac_ref, inv)
+        factorize(gram, fac_ref, inv, starts[:1])
+
+    def first_stage(par, d, begin):
+        z = lax.rem(my_z + d, deep)
+        for e in range(1, wide):
+            y = lax.rem(my_y + e, wide)
+            chunk = z * wide + y
+            slot = my_y * deep + z if begin else y * deep + z
+            copy = remote(
+                rs_out.at[chunk], rs_in.at[par, slot],
+                rs_send.at[par, chunk], rs_recv.at[par, slot], (my_row, my_z * wide + y),
+            )
+            copy.start() if begin else copy.wait()
+
+    def first_sum(par, d):
+        z = lax.rem(my_z + d, deep)
+        total = rs_out[z * wide + my_y].astype(F32)
+        for e in range(1, wide):
+            y = lax.rem(my_y + e, wide)
+            total = total + rs_in[par, y * deep + z].astype(F32)
+        return total
+
+    def second_stage(par, d, begin):
+        z = lax.rem(my_z + d, deep)
+        slot = my_z if begin else z
+        copy = remote(
+            s2_out.at[z], s2_in.at[par, slot],
+            s2_send.at[par, z], s2_recv.at[par, slot], (my_row, z * wide + my_y),
+        )
+        copy.start() if begin else copy.wait()
 
     for step in range(ITERS):
         par, last = step % 2, (step + 1) % 2
@@ -219,12 +254,23 @@
 
         if step:
             gram_middle(last)
-        rs_in[par, my_col] = rs_out[my_col]
-        start_cols(rs_out, rs_in.at[par], rs_send.at[par], rs_recv.at[par], False)
+        depths = list(range(1, deep))
+        for d in depths + [0]:
+            first_stage(par, d, True)
         if step:
             gram_end(last)
-        wait_cols(rs_out, rs_in.at[par], rs_send.at[par], rs_recv.at[par], False)
-        own = column_sum(rs_in, par) * scale_of(my_row)
+        for d in depths:
+            first_stage(par, d, False)
+            s2_out[lax.rem(my_z + d, deep)] = first_sum(par, d).astype(BF16)
+            second_stage(par, d, True)
+        if step:
+            factorize(gram, fac_ref, inv, starts[1:])
+        first_stage(par, 0, False)
+        own = first_sum(par, 0)
+        for d in depths:
+            second_stage(par, d, False)
+            own = own + s2_in[par, lax.rem(my_z + d, deep)].astype(F32)
+        own = own * scale_of(my_row)
         if step:
             own = exact_dot(own, inv[...])
         image[...] = own
@@ -238,6 +284,7 @@
     gram_start(par)
     gram_middle(par)
     gram_end(par)
+    factorize(gram, fac_ref, inv, starts[1:])
     emb_ref[...] = exact_dot(image[...], inv[...])
 
 
@@ -272,9 +319,11 @@
             pltpu.VMEM((width, width), F32),
             pltpu.VMEM((width, width), F32),
             pltpu.VMEM((rows, width), F32),
+            pltpu.VMEM((min(DEEP, n_col), rows, width), BF16),
+            pltpu.VMEM((2, min(DEEP, n_col), rows, width), BF16),
             dma((n_row,)), dma((n_row,)), dma((2, n_row)), dma((2, n_row)),
             dma((2, n_col)), dma((2, n_col)), dma((2, n_col)), dma((2, n_col)),
-            dma((2, n_col)), dma((2, n_col)),
+            dma((2, n_col)), dma((2, n_col)), dma((2, min(DEEP, n_col))), dma((2, min(DEEP, n_col))),
         ],
         compiler_params=pltpu.CompilerParams(
             collective_id=0, has_side_effects=True, vmem_limit_bytes=VMEM_BYTES

time: 199 us -> 180 us (0.905)
  Pallas kernels: 191 us -> 172 us
    pallas_call x1, Pallas kernels: 191 us -> 172 us  [body(): pl.pallas_call(functools.partial(kernel, n_row, n_col, nodes), out_shape=...]
where the time goes in v3:
time: 180 us
  Pallas kernels  172 us (96%)
  local copies, waits for them, and re-layouts  7.29 us (4%)
    pallas_call x1, Pallas kernels, body(): pl.pallas_call(functools.partial(kernel, n_row, n_col, nodes), out_shape=...  172 us
    unnamed x3, local copies, waits for them, and re-layouts  4.67 us

profile of v3, /device:TPU:0, one launch (start us, length us, event | category | flops | bytes accessed | tf_op | source)
XLA Modules:
  0.0 180.2 jit_solution(8213957760251759008)
XLA Ops:
  0.6 1.3 pad.4.scale_ref
  1.9 1.4 copy.7.index_ref
  3.3 1.3 copy.8.count_ref
  4.6 172.3 %shard_map.68 = (f32[256,256]{1,0:T(8,128)}, f32[256,256]{1,0:T(8,128)}) custom-call(bf16[16,8,128,128]{3,2,1,0:T(8,128)(2,1)} %bitcast.3, s32[16,8]{1,0:T(8,128)} %copy.7.index_ref, s32[16,1]{1,0:T(8,128)} %copy.8.count_ref, bf16[256,256]{1,0:T(8,128)(2,1)} %basis_ref.1, f32[8,128]{1,0:T(8,128)} %pad.4.scale_ref), custom_call_target="tpu_custom_call" | custom-call | tf_op jit(solution)/shard_map/pallas_call | solution.py:300
  176.9 1.7 copy.11
  178.5 1.7 copy.12

commit v4 on v3

--- a/solution.py
+++ b/solution.py
@@ -141,13 +141,21 @@
             device_id=device, device_id_type=MESH,
         )
 
+    mate = my_row + 1 - 2 * lax.rem(my_row, 2)
+    same = [lax.rem(my_row + 2 * d, n_row) for d in range(1, n_row // 2)]
+
     def start_gather(buf, send, recv):
-        for r in row_peers:
+        for r in same + [mate]:
             remote(buf.at[my_row], buf.at[my_row], send.at[r], recv.at[my_row], (r, my_col)).start()
 
     def wait_gather(buf, send, recv):
-        for r in row_peers:
+        across = [r + 1 - 2 * lax.rem(r, 2) for r in same]
+        for r, a in zip(same, across):
             remote(buf.at[my_row], buf.at[r], send.at[r], recv.at[r], (r, my_col)).wait()
+            remote(buf.at[r], buf.at[r], send.at[a], recv.at[r], (mate, my_col)).start()
+        remote(buf.at[my_row], buf.at[mate], send.at[mate], recv.at[mate], (mate, my_col)).wait()
+        for r, a in zip(same, across):
+            remote(buf.at[r], buf.at[a], send.at[a], recv.at[a], (mate, my_col)).wait()
 
     def start_cols(src, dst, send, recv, own_src):
         for c in col_peers:

time: 180 us -> 175 us (0.972)
  Pallas kernels: 172 us -> 167 us
    pallas_call x1, Pallas kernels: 172 us -> 167 us  [body(): pl.pallas_call(functools.partial(kernel, n_row, n_col, nodes), out_shape=...]
where the time goes in v4:
time: 175 us; the launch traced here: 174 us
  Pallas kernels  167 us (95%)
  local copies, waits for them, and re-layouts  7.29 us (4%)
    pallas_call x1, Pallas kernels, body(): pl.pallas_call(functools.partial(kernel, n_row, n_col, nodes), out_shape=...  167 us
    unnamed x3, local copies, waits for them, and re-layouts  4.67 us

profile of v4, /device:TPU:0, one launch (start us, length us, event | category | flops | bytes accessed | tf_op | source)
XLA Modules:
  0.0 174.5 jit_solution(10100800342180543686)
XLA Ops:
  0.6 1.3 pad.4.scale_ref
  1.9 1.4 copy.7.index_ref
  3.3 1.3 copy.8.count_ref
  4.6 166.6 %shard_map.68 = (f32[256,256]{1,0:T(8,128)}, f32[256,256]{1,0:T(8,128)}) custom-call(bf16[16,8,128,128]{3,2,1,0:T(8,128)(2,1)} %bitcast.3, s32[16,8]{1,0:T(8,128)} %copy.7.index_ref, s32[16,1]{1,0:T(8,128)} %copy.8.count_ref, bf16[256,256]{1,0:T(8,128)(2,1)} %basis_ref.1, f32[8,128]{1,0:T(8,128)} %pad.4.scale_ref), custom_call_target="tpu_custom_call" | custom-call | tf_op jit(solution)/shard_map/pallas_call | solution.py:308
  171.1 1.7 copy.11
  172.8 1.7 copy.12
